TPU v7x, 32 devices: a whole 2x2x4 slice. The times are simulated.
32 devices in a mesh: grp: 4 (over y, core), dev: 8 (over z, x).
Axes of the slice: x: 2, y: 2, z: 4, core: 2. Of those that a mesh axis runs over, the one named last changes fastest.
Arguments:
- blocks: bfloat16 [4, 8, 12, 64, 1728], P('grp', 'dev'), may hold values from -0.75 to 0.75
- prolong: bfloat16 [4, 8, 12, 64, 256], P('grp', 'dev'), may hold values from -0.75 to 0.75
- block_cols: int32 [4, 8, 12, 27], P('grp', 'dev'), may hold values from -1 to 23, as said below
- fetch_rows: int32 [4, 8, 8, 3], P('grp', 'dev'), may hold values from 0 to 11
- tile_slot: int32 [4, 8, 12, 27], P('grp', 'dev'), may hold values from 0 to 3
- tile_owner: int32 [4, 8, 4], P('grp', 'dev'), may hold values from 0 to 31, as said below
- tile_place: int32 [4, 8, 4], P('grp', 'dev'), may hold values from 0 to 1
Outputs:
- coarse: float32 [4, 8, 2, 256, 256], P('grp', 'dev')
Inputs may be any that keep to these rules, and one draw needn't show every extreme that they name: `block_cols`: -1 marks a padded block slot; at most 243 slots of one device are not padding, exactly 243 on the first device. `tile_owner`: the 4 tiles of one device go to owners of distinct dev indices; at most 1 of them go to owners in one group, exactly 1 to the device's own group.
All inputs are finite; a program needn't handle non-finite values.
Results may differ from a plain program's by a relative error of at most 0.004.
Values may be sent and summed in bfloat16 or wider, within the bound.
A program may use at most 128 MiB of HBM per device.

v0:
```python
import functools

import jax
import jax.numpy as jnp
from jax import lax
from jax.experimental import pallas as pl
from jax.experimental.pallas import tpu as pltpu
from jax.sharding import PartitionSpec as P

BLOCK = 64
W = 256
K = 27
CT = 2
NCAP = 3


def pick(panels, ids):
    ones = (ids[..., None] == jnp.arange(panels.shape[0], dtype=jnp.int32)).astype(panels.dtype)
    return jnp.einsum(
        "...p,prw->...rw", ones, panels, preferred_element_type=jnp.float32
    ).astype(panels.dtype)


def plain_body(blocks, prolong, block_cols, fetch_rows, tile_slot, tile_owner, tile_place):
    dev_count = lax.axis_size("dev")
    grp_count = lax.axis_size("grp")
    panels = prolong[0, 0]
    chosen = fetch_rows[0, 0]
    outgoing = pick(panels, chosen)
    arrived = lax.all_to_all(outgoing, "dev", split_axis=0, concat_axis=0, tiled=True)
    arrived = arrived.reshape(dev_count * NCAP, BLOCK, W)
    owners = tile_owner[0, 0]
    places = tile_place[0, 0]
    local_count = owners.shape[0]
    tile_range = jnp.arange(local_count, dtype=jnp.int32)

    def one_row(running, item):
        block_row, panel_row, column_ids, slot_ids = item
        matrix = block_row.reshape(BLOCK, K, BLOCK)
        near_panels = pick(arrived, column_ids)
        product = jnp.einsum(
            "rkc,kcw->krw", matrix, near_panels, preferred_element_type=jnp.float32
        )
        product = jnp.where((column_ids >= 0)[:, None, None], product, 0.0).astype(jnp.bfloat16)
        outer_tile = jnp.einsum(
            "ra,krb->kab", panel_row, product, preferred_element_type=jnp.float32
        )
        selector = (slot_ids[:, None] == tile_range[None, :]).astype(jnp.float32)
        added = jnp.einsum("kt,kab->tab", selector, outer_tile, precision=lax.Precision.HIGHEST)
        return (running + added, None)

    running = jnp.zeros((local_count, W, W), jnp.float32)
    running, unused = lax.scan(
        one_row, running, (blocks[0, 0], panels, block_cols[0, 0], tile_slot[0, 0])
    )
    partial_value = running.astype(jnp.bfloat16)
    dev_target = owners % dev_count
    grp_target = owners // dev_count
    sending = jnp.zeros((dev_count, W, W), jnp.bfloat16).at[dev_target].set(partial_value)
    labels = jnp.full((dev_count,), -1, jnp.int32).at[dev_target].set(grp_target * CT + places)
    got_tiles, got_labels = (
        lax.all_to_all(sending, "dev", split_axis=0, concat_axis=0, tiled=True),
        lax.all_to_all(labels, "dev", split_axis=0, concat_axis=0, tiled=True),
    )
    spread = grp_count * CT
    keyed = jnp.where(got_labels >= 0, got_labels, spread)
    table = (
        jnp.zeros((spread, W, W), jnp.float32)
        .at[keyed]
        .add(got_tiles.astype(jnp.float32), mode="drop")
    )
    result = lax.psum_scatter(table, "grp", scatter_dimension=0, tiled=True)
    return result.reshape(1, 1, CT, W, W)


MESH = pl.DeviceIdType.MESH
HALVES = 2
LABEL_ROWS = 16


def kernel(
    n_grp, n_dev, prolong_ref, cols_ref, fetch_ref, slot_ref, owner_ref, place_ref, blocks_ref,
    out_ref,
    mat, fetched, stage1, spread, near, high, low, panels_t, part, stage2, got2, stage3, got3, mine,
    blocks_sem, send1, recv1, send2, recv2, send3, recv3,
):
    rows = blocks_ref.shape[0]
    slots = cols_ref.shape[1]
    tiles = owner_ref.shape[0]
    ncap = fetch_ref.shape[1]
    sub = BLOCK // LABEL_ROWS
    piece = ncap * sub + 1
    half = W // HALVES
    g = lax.axis_index("grp")
    d = lax.axis_index("dev")
    load = pltpu.make_async_copy(blocks_ref, mat, blocks_sem)
    load.start()

    barrier = pltpu.get_barrier_semaphore()
    for j in range(1, n_dev):
        pl.semaphore_signal(barrier, inc=1, device_id=(g, lax.rem(d + j, n_dev)), device_id_type=MESH)
    for j in range(1, n_grp):
        pl.semaphore_signal(barrier, inc=1, device_id=(lax.rem(g + j, n_grp), d), device_id_type=MESH)

    def tile_for(target):
        found = jnp.int32(tiles)
        label = jnp.int32(-1)
        for t in range(tiles):
            hit = lax.rem(owner_ref[t], n_dev) == target
            found = jnp.where(hit, t, found)
            label = jnp.where(hit, lax.div(owner_ref[t], n_dev) * CT + place_ref[t], label)
        return found, label

    def fill(where, target, base, label):
        for c in range(ncap):
            panel = prolong_ref[fetch_ref[target, c]]
            where[pl.ds(base + c * sub, sub)] = panel.reshape(sub, LABEL_ROWS, W)
        tag = jnp.full((1, LABEL_ROWS, W), label.astype(jnp.float32), jnp.float32)
        where[pl.ds(base + ncap * sub, 1)] = tag.astype(jnp.bfloat16)

    found = [None] * n_dev
    for j in range(n_dev):
        target = lax.rem(d + j, n_dev)
        found[j], label = tile_for(target)
        if j == 0:
            fill(fetched, target, d * piece, label)
        else:
            fill(stage1.at[j], target, 0, label)

    pl.semaphore_wait(barrier, n_dev - 1 + n_grp - 1)
    first = []
    for j in far_first(n_dev):
        copy = pltpu.make_async_remote_copy(
            src_ref=stage1.at[j],
            dst_ref=fetched.at[pl.ds(d * piece, piece)],
            send_sem=send1.at[j],
            recv_sem=recv1.at[j],
            device_id=(g, lax.rem(d + j, n_dev)),
            device_id_type=MESH,
        )
        copy.start()
        first.append(copy)

    panels_t[...] = prolong_ref[...].reshape(rows * BLOCK, W).T
    for h in range(HALVES):
        part[h, tiles] = jnp.zeros((half, W), jnp.bfloat16)
    load.wait()
    lane = lax.broadcasted_iota(jnp.int32, (1, 2 * BLOCK), 1)

    def place_blocks(i, unused):
        for k in range(0, slots, 2):
            width = min(2, slots - k) * BLOCK
            ids = [
                jnp.where(cols_ref[i, m] >= 0, slot_ref[i, m], -1)
                for m in range(k, min(k + 2, slots))
            ]
            ids = jnp.where(lane < BLOCK, ids[0], ids[-1])[:, :width]
            at = slice(k * BLOCK, k * BLOCK + width)
            values = mat[i, :, at]
            for t in range(tiles):
                mask = jnp.where(ids == t, 1.0, 0.0).astype(jnp.bfloat16)
                spread[i, t * BLOCK : (t + 1) * BLOCK, at] = values * mask
        return unused

    lax.fori_loop(0, rows, place_blocks, 0)
    for copy in first:
        copy.wait()

    def one_row(i, unused):
        for k in range(slots):
            col = jnp.maximum(cols_ref[i, k], 0)
            panel = fetched[pl.ds(col * sub + lax.div(col, ncap), sub)]
            near[k * BLOCK : (k + 1) * BLOCK, :] = panel.reshape(BLOCK, W)
        total = jnp.dot(spread[i], near[...], preferred_element_type=jnp.float32)
        top = total.astype(jnp.bfloat16)
        rest = (total - top.astype(jnp.float32)).astype(jnp.bfloat16)
        at = pl.ds(pl.multiple_of(i * BLOCK, BLOCK), BLOCK)
        for t in range(tiles):
            high[t, at, :] = top[t * BLOCK : (t + 1) * BLOCK]
            low[t, at, :] = rest[t * BLOCK : (t + 1) * BLOCK]
        return unused

    lax.fori_loop(0, rows, one_row, 0)

    second = []
    for h in range(HALVES):
        left = panels_t[h * half : (h + 1) * half, :]
        for t in range(tiles):
            value = jnp.dot(left, high[t], preferred_element_type=jnp.float32)
            value += jnp.dot(left, low[t], preferred_element_type=jnp.float32)
            part[h, t] = value.astype(jnp.bfloat16)
        copies = []
        for j in far_first(n_dev):
            stage2[h, j] = part[h, found[j]]
            copy = pltpu.make_async_remote_copy(
                src_ref=stage2.at[h, j],
                dst_ref=got2.at[h, j],
                send_sem=send2.at[h, j],
                recv_sem=recv2.at[h, j],
                device_id=(g, lax.rem(d + j, n_dev)),
                device_id_type=MESH,
            )
            copy.start()
            copies.append(copy)
        got2[h, 0] = part[h, found[0]]
        second.append(copies)

    labels = []
    for j in range(n_dev):
        source = lax.rem(d + n_dev - j, n_dev)
        tag = fetched[source * piece + ncap * sub]
        labels.append(jnp.max(tag.astype(jnp.float32)))

    third = []
    step = 32
    for h in range(HALVES):
        for copy in second[h]:
            copy.wait()
        copies = []
        for jj in list(range(1, n_grp)) + [0]:
            target = lax.rem(g + jj, n_grp)
            weights = [
                [
                    jnp.where(labels[j] == (target * CT + q).astype(jnp.float32), 1.0, 0.0)
                    for j in range(n_dev)
                ]
                for q in range(CT)
            ]

            def add_up(r, unused):
                at = pl.ds(pl.multiple_of(r * step, step), step)
                sums = [jnp.zeros((step, W), jnp.float32) for q in range(CT)]
                for j in range(n_dev):
                    value = got2[h, j, at, :].astype(jnp.float32)
                    for q in range(CT):
                        sums[q] = sums[q] + value * weights[q][j]
                for q in range(CT):
                    if jj == 0:
                        mine[h, q, at, :] = sums[q]
                    else:
                        stage3[h, jj, q, at, :] = sums[q].astype(jnp.bfloat16)
                return unused

            lax.fori_loop(0, half // step, add_up, 0)
            if jj:
                copy = pltpu.make_async_remote_copy(
                    src_ref=stage3.at[h, jj],
                    dst_ref=got3.at[h, jj],
                    send_sem=send3.at[h, jj],
                    recv_sem=recv3.at[h, jj],
                    device_id=(target, d),
                    device_id_type=MESH,
                )
                copy.start()
                copies.append(copy)
        third.append(copies)

    for h in range(HALVES):
        for copy in third[h]:
            copy.wait()
        for q in range(CT):
            value = mine[h, q]
            for jj in range(1, n_grp):
                value = value + got3[h, jj, q].astype(jnp.float32)
            out_ref[q, h * half : (h + 1) * half, :] = value


def far_first(n):
    return sorted(range(1, n), key=lambda j: -min(j, n - j))


def body(blocks, prolong, block_cols, fetch_rows, tile_slot, tile_owner, tile_place):
    n_grp, n_dev = lax.axis_size("grp"), lax.axis_size("dev")
    rows = blocks.shape[2]
    slots = block_cols.shape[3]
    tiles = tile_owner.shape[2]
    ncap = fetch_rows.shape[3]
    if rows * tiles * BLOCK * slots * BLOCK * 2 > 16 * 2**20 or tiles > n_dev:
        return plain_body(
            blocks, prolong, block_cols, fetch_rows, tile_slot, tile_owner, tile_place
        )
    piece = ncap * (BLOCK // LABEL_ROWS) + 1
    half = W // HALVES
    vmem = pl.BlockSpec(memory_space=pltpu.VMEM)
    smem = pl.BlockSpec(memory_space=pltpu.SMEM)
    bf16, f32 = jnp.bfloat16, jnp.float32
    dma = pltpu.SemaphoreType.DMA
    result = pl.pallas_call(
        functools.partial(kernel, n_grp, n_dev),
        out_shape=jax.ShapeDtypeStruct((CT, W, W), f32),
        in_specs=[vmem, smem, smem, smem, smem, smem, pl.BlockSpec(memory_space=pl.ANY)],
        out_specs=vmem,
        scratch_shapes=[
            pltpu.VMEM((rows, BLOCK, slots * BLOCK), bf16),
            pltpu.VMEM((n_dev * piece, LABEL_ROWS, W), bf16),
            pltpu.VMEM((n_dev, piece, LABEL_ROWS, W), bf16),
            pltpu.VMEM((rows, tiles * BLOCK, slots * BLOCK), bf16),
            pltpu.VMEM((slots * BLOCK, W), bf16),
            pltpu.VMEM((tiles, rows * BLOCK, W), bf16),
            pltpu.VMEM((tiles, rows * BLOCK, W), bf16),
            pltpu.VMEM((W, rows * BLOCK), bf16),
            pltpu.VMEM((HALVES, tiles + 1, half, W), bf16),
            pltpu.VMEM((HALVES, n_dev, half, W), bf16),
            pltpu.VMEM((HALVES, n_dev, half, W), bf16),
            pltpu.VMEM((HALVES, n_grp, CT, half, W), bf16),
            pltpu.VMEM((HALVES, n_grp, CT, half, W), bf16),
            pltpu.VMEM((HALVES, CT, half, W), f32),
            dma,
            dma((n_dev,)),
            dma((n_dev,)),
            dma((HALVES, n_dev)),
            dma((HALVES, n_dev)),
            dma((HALVES, n_grp)),
            dma((HALVES, n_grp)),
        ],
        compiler_params=pltpu.CompilerParams(
            collective_id=0, has_side_effects=True, vmem_limit_bytes=48 * 2**20
        ),
    )(
        prolong[0, 0], block_cols[0, 0], fetch_rows[0, 0], tile_slot[0, 0], tile_owner[0, 0],
        tile_place[0, 0], blocks[0, 0],
    )
    return result.reshape(1, 1, CT, W, W)


def solution(mesh):
    return jax.shard_map(
        body,
        mesh=mesh,
        in_specs=(
            P("grp", "dev", None, None, None),
            P("grp", "dev", None, None, None),
            P("grp", "dev", None, None),
            P("grp", "dev", None, None),
            P("grp", "dev", None, None),
            P("grp", "dev", None),
            P("grp", "dev", None),
        ),
        out_specs=P("grp", "dev", None, None, None),
        check_vma=False,
    )
```

profile of v0, /device:TPU:1, one launch (start us, length us, event | category | flops | bytes accessed | tf_op | source)
XLA Modules:
  0.0 65.6 jit_solution(9848968173010037562)
XLA Ops:
  0.0 0.8 %copy.9 = s32[1,1,8,3]{3,2,1,0:T(8,128)S(1)} copy(s32[1,1,8,3]{2,1,3,0:T(1,128)} %param.10) | data formatting | bytes 192 | tf_op jit(solution)/shard_map/squeeze | solution.py:320
  0.8 0.7 %copy_bitcast_fusion = (s32[12,27]{1,0:T(8,128)S(1)}, s32[12,27]{1,0:T(8,128)S(1)}) fusion(s32[1,1,12,27]{3,1,2,0:T(1,128)} %param.11, s32[1,1,12,27]{3,1,2,0:T(1,128)} %param.9), kind=kLoop, calls=%fused_computation | loop fusion | bytes 5184
  1.5 0.0 copy-start
  1.5 1.8 %copy-done = bf16[1,1,12,64,1728]{4,3,2,1,0:T(8,128)(2,1)S(1)} copy-done((bf16[1,1,12,64,1728]{4,3,2,1,0:T(8,128)(2,1)S(1)}, bf16[1,1,12,64,1728]{4,3,2,1,0:T(8,128)(2,1)}, u32[]{:S(2)}) %copy-start) | copy-done | bytes 2654232
  3.2 0.0 copy-start.1
  3.2 1.0 %copy-done.1 = bf16[1,1,12,64,256]{4,3,2,1,0:T(8,128)(2,1)S(1)} copy-done((bf16[1,1,12,64,256]{4,3,2,1,0:T(8,128)(2,1)S(1)}, bf16[1,1,12,64,256]{4,3,2,1,0:T(8,128)(2,1)}, u32[]{:S(2)}) %copy-start.1) | copy-done | bytes 393240
  4.2 0.0 copy-start.2
  4.2 0.7 copy-done.2
  4.9 0.0 copy-start.3
  4.9 0.7 copy-done.3
  5.6 59.2 %shard_map.73 = f32[2,256,256]{2,1,0:T(8,128)S(1)} custom-call(bf16[12,64,256]{2,1,0:T(8,128)(2,1)S(1)} %bitcast.12, s32[12,27]{1,0:T(8,128)S(1)} %get-tuple-element.6.cols_ref, s32[8,3]{1,0:T(8,128)S(1)} %bitcast.13, s32[12,27]{1,0:T(8,128)S(1)} %get-tuple-element.5.slot_ref, s32[4]{0:T(128)S(1)} %bitcast.14, s32[4]{0:T(128)S(1)} %bitcast.15, ...), custom_call_target="tpu_custom_call" | custom-call | tf_op jit(solution)/shard_map/pallas_call | solution.py:288
  64.8 0.8 %copy.15 = f32[1,1,2,256,256]{4,3,2,1,0:T(8,128)} copy(f32[1,1,2,256,256]{4,3,2,1,0:T(8,128)S(1)} %bitcast.11) | data formatting | bytes 1048576
Async XLA Ops:
  1.5 1.8 %copy-start = (bf16[1,1,12,64,1728]{4,3,2,1,0:T(8,128)(2,1)S(1)}, bf16[1,1,12,64,1728]{4,3,2,1,0:T(8,128)(2,1)}, u32[]{:S(2)}) copy-start(bf16[1,1,12,64,1728]{4,3,2,1,0:T(8,128)(2,1)} %param.7) | copy-start | bytes 7962628
  3.2 1.0 %copy-start.1 = (bf16[1,1,12,64,256]{4,3,2,1,0:T(8,128)(2,1)S(1)}, bf16[1,1,12,64,256]{4,3,2,1,0:T(8,128)(2,1)}, u32[]{:S(2)}) copy-start(bf16[1,1,12,64,256]{4,3,2,1,0:T(8,128)(2,1)} %param.8) | copy-start | bytes 1179652
  4.2 0.7 copy-start.2
  4.9 0.7 copy-start.3
where the time goes:
time: 66.1 us; the launch traced here: 65.6 us
  Pallas kernels  59.2 us (90%)
  local copies, waits for them, and re-layouts  6.34 us (10%)
    pallas_call x1, Pallas kernels, body(): pl.pallas_call(functools.partial(kernel, n_grp, n_dev), out_shape=jax.Sha...  59.2 us
    unnamed x10, local copies, waits for them, and re-layouts  5.59 us

commit v1 on v0

v1 whole, which is shorter than its diff:
```python
import functools

import jax
import jax.numpy as jnp
from jax import lax
from jax.experimental import pallas as pl
from jax.experimental.pallas import tpu as pltpu
from jax.sharding import PartitionSpec as P

BLOCK = 64
W = 256
K = 27
CT = 2
NCAP = 3


def pick(panels, ids):
    ones = (ids[..., None] == jnp.arange(panels.shape[0], dtype=jnp.int32)).astype(panels.dtype)
    return jnp.einsum(
        "...p,prw->...rw", ones, panels, preferred_element_type=jnp.float32
    ).astype(panels.dtype)


def plain_body(blocks, prolong, block_cols, fetch_rows, tile_slot, tile_owner, tile_place):
    dev_count = lax.axis_size("dev")
    grp_count = lax.axis_size("grp")
    panels = prolong[0, 0]
    chosen = fetch_rows[0, 0]
    outgoing = pick(panels, chosen)
    arrived = lax.all_to_all(outgoing, "dev", split_axis=0, concat_axis=0, tiled=True)
    arrived = arrived.reshape(dev_count * NCAP, BLOCK, W)
    owners = tile_owner[0, 0]
    places = tile_place[0, 0]
    local_count = owners.shape[0]
    tile_range = jnp.arange(local_count, dtype=jnp.int32)

    def one_row(running, item):
        block_row, panel_row, column_ids, slot_ids = item
        matrix = block_row.reshape(BLOCK, K, BLOCK)
        near_panels = pick(arrived, column_ids)
        product = jnp.einsum(
            "rkc,kcw->krw", matrix, near_panels, preferred_element_type=jnp.float32
        )
        product = jnp.where((column_ids >= 0)[:, None, None], product, 0.0).astype(jnp.bfloat16)
        outer_tile = jnp.einsum(
            "ra,krb->kab", panel_row, product, preferred_element_type=jnp.float32
        )
        selector = (slot_ids[:, None] == tile_range[None, :]).astype(jnp.float32)
        added = jnp.einsum("kt,kab->tab", selector, outer_tile, precision=lax.Precision.HIGHEST)
        return (running + added, None)

    running = jnp.zeros((local_count, W, W), jnp.float32)
    running, unused = lax.scan(
        one_row, running, (blocks[0, 0], panels, block_cols[0, 0], tile_slot[0, 0])
    )
    partial_value = running.astype(jnp.bfloat16)
    dev_target = owners % dev_count
    grp_target = owners // dev_count
    sending = jnp.zeros((dev_count, W, W), jnp.bfloat16).at[dev_target].set(partial_value)
    labels = jnp.full((dev_count,), -1, jnp.int32).at[dev_target].set(grp_target * CT + places)
    got_tiles, got_labels = (
        lax.all_to_all(sending, "dev", split_axis=0, concat_axis=0, tiled=True),
        lax.all_to_all(labels, "dev", split_axis=0, concat_axis=0, tiled=True),
    )
    spread = grp_count * CT
    keyed = jnp.where(got_labels >= 0, got_labels, spread)
    table = (
        jnp.zeros((spread, W, W), jnp.float32)
        .at[keyed]
        .add(got_tiles.astype(jnp.float32), mode="drop")
    )
    result = lax.psum_scatter(table, "grp", scatter_dimension=0, tiled=True)
    return result.reshape(1, 1, CT, W, W)


MESH = pl.DeviceIdType.MESH
HALVES = 2
CUTS = 2
LABEL_ROWS = 16


def kernel(
    n_grp, n_dev, cols_ref, fetch_ref, slot_ref, owner_ref, place_ref, prolong_hbm, blocks_hbm,
    out_ref,
    prolong_ref, mat, fetched_a, fetched_b, stage1, spread, near, high, low, panels_t, part, stage2, got2,
    stage3, got3, mine,
    prolong_sem, blocks_sem, send1, recv1, send2, recv2, send3, recv3,
):
    rows = blocks_hbm.shape[0]
    slots = cols_ref.shape[2]
    tiles = owner_ref.shape[0]
    ncap = fetch_ref.shape[0]
    sub = BLOCK // LABEL_ROWS
    piece = ncap * sub + 1
    wide = W // HALVES
    tall = W // CUTS
    g = lax.axis_index("grp")
    d = lax.axis_index("dev")
    fetched = (fetched_a, fetched_b)
    first_load = pltpu.make_async_copy(prolong_hbm, prolong_ref, prolong_sem)
    first_load.start()
    load = pltpu.make_async_copy(blocks_hbm, mat, blocks_sem)
    load.start()

    barrier = pltpu.get_barrier_semaphore()
    for j in range(1, n_dev):
        pl.semaphore_signal(barrier, inc=1, device_id=(g, lax.rem(d + j, n_dev)), device_id_type=MESH)
    for j in range(1, n_grp):
        pl.semaphore_signal(barrier, inc=1, device_id=(lax.rem(g + j, n_grp), d), device_id_type=MESH)

    def tile_for(target):
        found = jnp.int32(tiles)
        label = jnp.int32(-1)
        for t in range(tiles):
            hit = lax.rem(owner_ref[t], n_dev) == target
            found = jnp.where(hit, t, found)
            label = jnp.where(hit, lax.div(owner_ref[t], n_dev) * CT + place_ref[t], label)
        return found, label

    def fill(where, target, base, label):
        tag = jnp.full((1, LABEL_ROWS, wide), label.astype(jnp.float32), jnp.float32)
        tag = tag.astype(jnp.bfloat16)
        for c in range(ncap):
            panel = prolong_ref[fetch_ref[c, 0, target]]
            for h in range(HALVES):
                half = panel[:, h * wide : (h + 1) * wide]
                where[h][pl.ds(base + c * sub, sub)] = half.reshape(sub, LABEL_ROWS, wide)
        for h in range(HALVES):
            where[h][pl.ds(base + ncap * sub, 1)] = tag

    first_load.wait()
    found = [None] * n_dev
    labels = [None] * n_dev
    for j in range(n_dev):
        found[j], labels[j] = tile_for(lax.rem(d + j, n_dev))
    first = [[] for h in range(HALVES)]
    order = far_first(n_dev)

    def send_panels(h, j):
        copy = pltpu.make_async_remote_copy(
            src_ref=stage1.at[j, h],
            dst_ref=fetched[h].at[pl.ds(d * piece, piece)],
            send_sem=send1.at[h, j],
            recv_sem=recv1.at[h, j],
            device_id=(g, lax.rem(d + j, n_dev)),
            device_id_type=MESH,
        )
        copy.start()
        first[h].append(copy)

    for j in order:
        fill([stage1.at[j, h] for h in range(HALVES)], lax.rem(d + j, n_dev), 0, labels[j])
        if j == order[0]:
            pl.semaphore_wait(barrier, n_dev - 1 + n_grp - 1)
        send_panels(0, j)
    for h in range(1, HALVES):
        for j in order:
            send_panels(h, j)
    fill(fetched, d, d * piece, labels[0])

    panels_t[...] = prolong_ref[...].reshape(rows * BLOCK, W).T
    for h in range(HALVES):
        part[h, tiles] = jnp.zeros((W, wide), jnp.bfloat16)
    load.wait()
    lane = lax.broadcasted_iota(jnp.int32, (1, 2 * BLOCK), 1)

    def place_blocks(i, unused):
        for k in range(0, slots, 2):
            width = min(2, slots - k) * BLOCK
            ids = [
                jnp.where(cols_ref[i, 0, m] >= 0, slot_ref[i, 0, m], -1)
                for m in range(k, min(k + 2, slots))
            ]
            ids = jnp.where(lane < BLOCK, ids[0], ids[-1])[:, :width]
            at = slice(k * BLOCK, k * BLOCK + width)
            values = mat[i, :, at]
            for t in range(tiles):
                mask = jnp.where(ids == t, 1.0, 0.0).astype(jnp.bfloat16)
                spread[i, t * BLOCK : (t + 1) * BLOCK, at] = values * mask
        return unused

    lax.fori_loop(0, rows, place_blocks, 0)

    second = []
    for h in range(HALVES):
        for copy in first[h]:
            copy.wait()

        def one_row(i, unused):
            for k in range(slots):
                col = jnp.maximum(cols_ref[i, 0, k], 0)
                panel = fetched[h][pl.ds(col * sub + lax.div(col, ncap), sub)]
                near[k * BLOCK : (k + 1) * BLOCK, :] = panel.reshape(BLOCK, wide)
            total = jnp.dot(spread[i], near[...], preferred_element_type=jnp.float32)
            top = total.astype(jnp.bfloat16)
            rest = (total - top.astype(jnp.float32)).astype(jnp.bfloat16)
            at = pl.ds(pl.multiple_of(i * BLOCK, BLOCK), BLOCK)
            for t in range(tiles):
                mine_at = slice(t * wide, (t + 1) * wide)
                high[at, mine_at] = top[t * BLOCK : (t + 1) * BLOCK]
                low[at, mine_at] = rest[t * BLOCK : (t + 1) * BLOCK]
            return unused

        lax.fori_loop(0, rows, one_row, 0)

        for v in range(CUTS):
            down = slice(v * tall, (v + 1) * tall)
            left = panels_t[down, :]
            value = jnp.dot(left, high[...], preferred_element_type=jnp.float32)
            value += jnp.dot(left, low[...], preferred_element_type=jnp.float32)
            for t in range(tiles):
                part[h, t, down, :] = value[:, t * wide : (t + 1) * wide].astype(jnp.bfloat16)
            copies = []
            for j in order:
                stage2[h, v, j] = part[h, found[j], down, :]
                copy = pltpu.make_async_remote_copy(
                    src_ref=stage2.at[h, v, j],
                    dst_ref=got2.at[h, v, j],
                    send_sem=send2.at[h, v, j],
                    recv_sem=recv2.at[h, v, j],
                    device_id=(g, lax.rem(d + j, n_dev)),
                    device_id_type=MESH,
                )
                copy.start()
                copies.append(copy)
            got2[h, v, 0] = part[h, found[0], down, :]
            second.append(copies)

    marks = []
    for j in range(n_dev):
        source = lax.rem(d + n_dev - j, n_dev)
        tag = fetched[0][source * piece + ncap * sub]
        marks.append(jnp.max(tag.astype(jnp.float32)))

    third = []
    step = 32
    for n in range(HALVES * CUTS):
        h, v = n // CUTS, n % CUTS
        for copy in second[n]:
            copy.wait()
        copies = []
        for jj in list(range(1, n_grp)) + [0]:
            target = lax.rem(g + jj, n_grp)
            weights = [
                [
                    jnp.where(marks[j] == (target * CT + q).astype(jnp.float32), 1.0, 0.0)
                    for j in range(n_dev)
                ]
                for q in range(CT)
            ]

            def add_up(r, unused):
                at = pl.ds(pl.multiple_of(r * step, step), step)
                sums = [jnp.zeros((step, wide), jnp.float32) for q in range(CT)]
                for j in range(n_dev):
                    value = got2[h, v, j, at, :].astype(jnp.float32)
                    for q in range(CT):
                        sums[q] = sums[q] + value * weights[q][j]
                for q in range(CT):
                    if jj == 0:
                        mine[h, v, q, at, :] = sums[q]
                    else:
                        stage3[h, v, jj, q, at, :] = sums[q].astype(jnp.bfloat16)
                return unused

            lax.fori_loop(0, tall // step, add_up, 0)
            if jj:
                copy = pltpu.make_async_remote_copy(
                    src_ref=stage3.at[h, v, jj],
                    dst_ref=got3.at[h, v, jj],
                    send_sem=send3.at[h, v, jj],
                    recv_sem=recv3.at[h, v, jj],
                    device_id=(target, d),
                    device_id_type=MESH,
                )
                copy.start()
                copies.append(copy)
        third.append(copies)

    for n in range(HALVES * CUTS):
        h, v = n // CUTS, n % CUTS
        for copy in third[n]:
            copy.wait()
        for q in range(CT):
            value = mine[h, v, q]
            for jj in range(1, n_grp):
                value = value + got3[h, v, jj, q].astype(jnp.float32)
            out_ref[q, v * tall : (v + 1) * tall, h * wide : (h + 1) * wide] = value


def far_first(n):
    return sorted(range(1, n), key=lambda j: -min(j, n - j))


def body(blocks, prolong, block_cols, fetch_rows, tile_slot, tile_owner, tile_place):
    n_grp, n_dev = lax.axis_size("grp"), lax.axis_size("dev")
    rows = blocks.shape[2]
    slots = block_cols.shape[3]
    tiles = tile_owner.shape[2]
    ncap = fetch_rows.shape[3]
    if rows * tiles * BLOCK * slots * BLOCK * 2 > 16 * 2**20 or tiles > n_dev:
        return plain_body(
            blocks, prolong, block_cols, fetch_rows, tile_slot, tile_owner, tile_place
        )
    piece = ncap * (BLOCK // LABEL_ROWS) + 1
    wide, tall = W // HALVES, W // CUTS
    vmem = pl.BlockSpec(memory_space=pltpu.VMEM)
    smem = pl.BlockSpec(memory_space=pltpu.SMEM)
    bf16, f32 = jnp.bfloat16, jnp.float32
    dma = pltpu.SemaphoreType.DMA
    result = pl.pallas_call(
        functools.partial(kernel, n_grp, n_dev),
        out_shape=jax.ShapeDtypeStruct((CT, W, W), f32),
        in_specs=[smem] * 5 + [pl.BlockSpec(memory_space=pltpu.HBM)] * 2,
        out_specs=vmem,
        scratch_shapes=[
            pltpu.VMEM((rows, BLOCK, W), bf16),
            pltpu.VMEM((rows, BLOCK, slots * BLOCK), bf16),
            pltpu.VMEM((n_dev * piece, LABEL_ROWS, wide), bf16),
            pltpu.VMEM((n_dev * piece, LABEL_ROWS, wide), bf16),
            pltpu.VMEM((n_dev, HALVES, piece, LABEL_ROWS, wide), bf16),
            pltpu.VMEM((rows, tiles * BLOCK, slots * BLOCK), bf16),
            pltpu.VMEM((slots * BLOCK, wide), bf16),
            pltpu.VMEM((rows * BLOCK, tiles * wide), bf16),
            pltpu.VMEM((rows * BLOCK, tiles * wide), bf16),
            pltpu.VMEM((W, rows * BLOCK), bf16),
            pltpu.VMEM((HALVES, tiles + 1, W, wide), bf16),
            pltpu.VMEM((HALVES, CUTS, n_dev, tall, wide), bf16),
            pltpu.VMEM((HALVES, CUTS, n_dev, tall, wide), bf16),
            pltpu.VMEM((HALVES, CUTS, n_grp, CT, tall, wide), bf16),
            pltpu.VMEM((HALVES, CUTS, n_grp, CT, tall, wide), bf16),
            pltpu.VMEM((HALVES, CUTS, CT, tall, wide), f32),
            dma,
            dma,
            dma((HALVES, n_dev)),
            dma((HALVES, n_dev)),
            dma((HALVES, CUTS, n_dev)),
            dma((HALVES, CUTS, n_dev)),
            dma((HALVES, CUTS, n_grp)),
            dma((HALVES, CUTS, n_grp)),
        ],
        compiler_params=pltpu.CompilerParams(
            collective_id=0, has_side_effects=True, vmem_limit_bytes=62 * 2**20
        ),
    )(
        block_cols[0].transpose(1, 0, 2), fetch_rows[0].transpose(2, 0, 1), tile_slot[0].transpose(1, 0, 2),
        tile_owner[0, 0], tile_place[0, 0], prolong[0, 0], blocks[0, 0],
    )
    return result.reshape(1, 1, CT, W, W)


def solution(mesh):
    return jax.shard_map(
        body,
        mesh=mesh,
        in_specs=(
            P("grp", "dev", None, None, None),
            P("grp", "dev", None, None, None),
            P("grp", "dev", None, None),
            P("grp", "dev", None, None),
            P("grp", "dev", None, None),
            P("grp", "dev", None),
            P("grp", "dev", None),
        ),
        out_specs=P("grp", "dev", None, None, None),
        check_vma=False,
    )
```

time: 66.1 us -> 56.1 us (0.85)
  Pallas kernels: 59.2 us -> 54 us
  local copies, waits for them, and re-layouts: 6.34 us -> 1.87 us
    pallas_call x1, Pallas kernels: 59.2 us -> 54 us  [body(): pl.pallas_call(functools.partial(kernel, n_grp, n_dev), out_shape=jax.Sha...]
    unnamed x10 -> x1, local copies, waits for them, and re-layouts: 5.59 us -> 1.87 us
    squeeze x1 -> x0, local copies, waits for them, and re-layouts: 0.75 us -> none  [body(): fetch_rows[0, 0]]
where the time goes in v1:
time: 56.1 us; the launch traced here: 55.9 us
  Pallas kernels  54 us (96%)
  local copies, waits for them, and re-layouts  1.87 us (3%)
    pallas_call x1, Pallas kernels, body(): pl.pallas_call(functools.partial(kernel, n_grp, n_dev), out_shape=jax.Sha...  54 us
    unnamed x1, local copies, waits for them, and re-layouts  1.87 us

profile of v1, /device:TPU:1, one launch (start us, length us, event | category | flops | bytes accessed | tf_op | source)
XLA Modules:
  0.0 55.9 jit_solution(11174817455858859264)
XLA Ops:
  0.0 54.0 %shard_map.73 = f32[2,256,256]{2,1,0:T(8,128)} custom-call(s32[12,1,27]{2,1,0:T(1,128)} %bitcast.13, s32[3,1,8]{2,1,0:T(1,128)} %bitcast.15, s32[12,1,27]{2,1,0:T(1,128)} %bitcast.14, s32[4]{0:T(128)} %bitcast.16, s32[4]{0:T(128)} %bitcast.17, bf16[12,64,256]{2,1,0:T(8,128)(2,1)} %bitcast.12, bf16[12,64,1728]{2,1,0:T(8,128)(2,1)} %bitcast.10), custom_call_target="tpu_custom_call" | custom-call | tf_op jit(solution)/shard_map/pallas_call | solution.py:311
  54.0 1.9 %copy.9 = f32[1,1,2,256,256]{4,3,2,1,0:T(8,128)} copy(f32[1,1,2,256,256]{4,3,2,1,0:T(8,128)} %bitcast.11) | data formatting | bytes 1048576

commit v2 on v1

--- a/solution.py
+++ b/solution.py
@@ -80,11 +80,12 @@
 
 
 def kernel(
-    n_grp, n_dev, cols_ref, fetch_ref, slot_ref, owner_ref, place_ref, prolong_hbm, blocks_hbm,
-    out_ref,
+    n_grp, n_dev, cols_hbm, fetch_hbm, slot_hbm, owner_hbm, place_hbm, prolong_hbm, blocks_hbm,
+    out_hbm,
+    cols_ref, fetch_ref, slot_ref, owner_ref, place_ref, out_ref,
     prolong_ref, mat, fetched_a, fetched_b, stage1, spread, near, high, low, panels_t, part, stage2, got2,
     stage3, got3, mine,
-    prolong_sem, blocks_sem, send1, recv1, send2, recv2, send3, recv3,
+    prolong_sem, blocks_sem, ids_sem, out_sem, send1, recv1, send2, recv2, send3, recv3,
 ):
     rows = blocks_hbm.shape[0]
     slots = cols_ref.shape[2]
@@ -97,6 +98,17 @@
     g = lax.axis_index("grp")
     d = lax.axis_index("dev")
     fetched = (fetched_a, fetched_b)
+    id_loads = [
+        pltpu.make_async_copy(source, target, ids_sem.at[n])
+        for n, (source, target) in enumerate(
+            (
+                (fetch_hbm, fetch_ref), (owner_hbm, owner_ref), (place_hbm, place_ref),
+                (cols_hbm, cols_ref), (slot_hbm, slot_ref),
+            )
+        )
+    ]
+    for copy in id_loads:
+        copy.start()
     first_load = pltpu.make_async_copy(prolong_hbm, prolong_ref, prolong_sem)
     first_load.start()
     load = pltpu.make_async_copy(blocks_hbm, mat, blocks_sem)
@@ -128,6 +140,8 @@
         for h in range(HALVES):
             where[h][pl.ds(base + ncap * sub, 1)] = tag
 
+    for copy in id_loads:
+        copy.wait()
     first_load.wait()
     found = [None] * n_dev
     labels = [None] * n_dev
@@ -277,6 +291,7 @@
                 copies.append(copy)
         third.append(copies)
 
+    saves = []
     for n in range(HALVES * CUTS):
         h, v = n // CUTS, n % CUTS
         for copy in third[n]:
@@ -285,7 +300,16 @@
             value = mine[h, v, q]
             for jj in range(1, n_grp):
                 value = value + got3[h, v, jj, q].astype(jnp.float32)
-            out_ref[q, v * tall : (v + 1) * tall, h * wide : (h + 1) * wide] = value
+            out_ref[n, q] = value
+        save = pltpu.make_async_copy(
+            out_ref.at[n],
+            out_hbm.at[:, pl.ds(v * tall, tall), pl.ds(h * wide, wide)],
+            out_sem.at[n],
+        )
+        save.start()
+        saves.append(save)
+    for save in saves:
+        save.wait()
 
 
 def far_first(n):
@@ -304,16 +328,20 @@
         )
     piece = ncap * (BLOCK // LABEL_ROWS) + 1
     wide, tall = W // HALVES, W // CUTS
-    vmem = pl.BlockSpec(memory_space=pltpu.VMEM)
-    smem = pl.BlockSpec(memory_space=pltpu.SMEM)
     bf16, f32 = jnp.bfloat16, jnp.float32
     dma = pltpu.SemaphoreType.DMA
     result = pl.pallas_call(
         functools.partial(kernel, n_grp, n_dev),
         out_shape=jax.ShapeDtypeStruct((CT, W, W), f32),
-        in_specs=[smem] * 5 + [pl.BlockSpec(memory_space=pltpu.HBM)] * 2,
-        out_specs=vmem,
+        in_specs=[pl.BlockSpec(memory_space=pl.ANY)] * 7,
+        out_specs=pl.BlockSpec(memory_space=pl.ANY),
         scratch_shapes=[
+            pltpu.SMEM((rows, 1, slots), jnp.int32),
+            pltpu.SMEM((ncap, 1, n_dev), jnp.int32),
+            pltpu.SMEM((rows, 1, slots), jnp.int32),
+            pltpu.SMEM((tiles,), jnp.int32),
+            pltpu.SMEM((tiles,), jnp.int32),
+            pltpu.VMEM((HALVES * CUTS, CT, tall, wide), f32),
             pltpu.VMEM((rows, BLOCK, W), bf16),
             pltpu.VMEM((rows, BLOCK, slots * BLOCK), bf16),
             pltpu.VMEM((n_dev * piece, LABEL_ROWS, wide), bf16),
@@ -332,6 +360,8 @@
             pltpu.VMEM((HALVES, CUTS, CT, tall, wide), f32),
             dma,
             dma,
+            dma((5,)),
+            dma((HALVES * CUTS,)),
             dma((HALVES, n_dev)),
             dma((HALVES, n_dev)),
             dma((HALVES, CUTS, n_dev)),

time: 56.1 us -> 55 us (0.980)
  Pallas kernels: 54 us -> 53 us
    pallas_call x1, Pallas kernels: 54 us -> 53 us  [body(): pl.pallas_call(functools.partial(kernel, n_grp, n_dev), out_shape=jax.Sha...]
where the time goes in v2:
time: 55 us; the launch traced here: 54.9 us
  Pallas kernels  53 us (96%)
  local copies, waits for them, and re-layouts  1.87 us (3%)
    pallas_call x1, Pallas kernels, body(): pl.pallas_call(functools.partial(kernel, n_grp, n_dev), out_shape=jax.Sha...  53 us
    unnamed x1, local copies, waits for them, and re-layouts  1.87 us

profile of v2, /device:TPU:1, one launch (start us, length us, event | category | flops | bytes accessed | tf_op | source)
XLA Modules:
  0.0 54.9 jit_solution(6616593259579603694)
XLA Ops:
  0.0 53.0 %shard_map.73 = f32[2,256,256]{2,1,0:T(8,128)} custom-call(s32[12,1,27]{2,1,0:T(1,128)} %bitcast.13, s32[3,1,8]{2,1,0:T(1,128)} %bitcast.15, s32[12,1,27]{2,1,0:T(1,128)} %bitcast.14, s32[4]{0:T(128)} %bitcast.16, s32[4]{0:T(128)} %bitcast.17, bf16[12,64,256]{2,1,0:T(8,128)(2,1)} %bitcast.12, bf16[12,64,1728]{2,1,0:T(8,128)(2,1)} %bitcast.10), custom_call_target="tpu_custom_call" | custom-call | tf_op jit(solution)/shard_map/pallas_call | solution.py:333
  53.0 1.9 %copy.9 = f32[1,1,2,256,256]{4,3,2,1,0:T(8,128)} copy(f32[1,1,2,256,256]{4,3,2,1,0:T(8,128)} %bitcast.11) | data formatting | bytes 1048576

commit v3 on v2

--- a/solution.py
+++ b/solution.py
@@ -75,7 +75,7 @@
 
 MESH = pl.DeviceIdType.MESH
 HALVES = 2
-CUTS = 2
+CUTS = 4
 LABEL_ROWS = 16
 
 

time: 55 us -> 55.7 us (1.013)
  no operation moved by 1% of the time
where the time goes in v3:
time: 55.7 us; the launch traced here: 55.3 us
  Pallas kernels  53.4 us (96%)
  local copies, waits for them, and re-layouts  1.87 us (3%)
    pallas_call x1, Pallas kernels, body(): pl.pallas_call(functools.partial(kernel, n_grp, n_dev), out_shape=jax.Sha...  53.4 us
    unnamed x1, local copies, waits for them, and re-layouts  1.87 us

profile of v3, /device:TPU:1, one launch (start us, length us, event | category | flops | bytes accessed | tf_op | source)
XLA Modules:
  0.0 55.3 jit_solution(523017110022418272)
XLA Ops:
  0.0 53.4 %shard_map.73 = f32[2,256,256]{2,1,0:T(8,128)} custom-call(s32[12,1,27]{2,1,0:T(1,128)} %bitcast.13, s32[3,1,8]{2,1,0:T(1,128)} %bitcast.15, s32[12,1,27]{2,1,0:T(1,128)} %bitcast.14, s32[4]{0:T(128)} %bitcast.16, s32[4]{0:T(128)} %bitcast.17, bf16[12,64,256]{2,1,0:T(8,128)(2,1)} %bitcast.12, bf16[12,64,1728]{2,1,0:T(8,128)(2,1)} %bitcast.10), custom_call_target="tpu_custom_call" | custom-call | tf_op jit(solution)/shard_map/pallas_call | solution.py:333
  53.4 1.9 %copy.9 = f32[1,1,2,256,256]{4,3,2,1,0:T(8,128)} copy(f32[1,1,2,256,256]{4,3,2,1,0:T(8,128)} %bitcast.11) | data formatting | bytes 1048576
